TPU v7x, 128 devices: a whole 4x4x4 slice. The times are simulated.
128 devices in a mesh: row: 8 (over y, z_hi), col: 16 (over z_lo, x, core).
Axes of the slice: x: 4, y: 4, z: 4 (z_hi: 2, z_lo: 2; z = z_hi * 2 + z_lo), core: 2. Of those that a mesh axis runs over, the one named last changes fastest.
Arguments:
- pair_rows: float32 [768, 768, 128], P(('row', 'col')), may hold values from -6 to 6
- valid_count: int32 [1], replicated, may hold values from 384 to 767
- start_proj: float32 [4, 128, 128], replicated, may hold values from -0.9 to 0.9
- start_out: float32 [128, 128], replicated, may hold values from -0.72 to 0.72
- start_bias: float32 [128, 4], replicated, may hold values from -1.08 to 1.08
- end_proj: float32 [4, 128, 128], replicated, may hold values from -0.9 to 0.9
- end_out: float32 [128, 128], replicated, may hold values from -0.72 to 0.72
- end_bias: float32 [128, 4], replicated, may hold values from -1.08 to 1.08
Outputs:
- pair_out: float32 [768, 768, 128], P(('row', 'col'))
All inputs are finite; a program needn't handle non-finite values.
Results may differ from a plain program's by a relative error of at most 0.00007.
Values sent between devices are 32-bit elements; how exact they have to be, the bound alone decides.
No kernel may reach another device: no remote copies, remote signals or barrier semaphores. Data moves between devices by JAX's collectives and lax.ppermute only.
A program may use at most 128 MiB of HBM per device.

v0:
```python
import jax
import jax.numpy as jnp
from jax import lax
from jax.sharding import PartitionSpec as P

HIGHEST = lax.Precision.HIGHEST
MASKED = -1000000000.0


def layer_norm(values):
    average = jnp.mean(values, axis=-1, keepdims=True)
    centred = values - average
    variance = jnp.mean(centred * centred, axis=-1, keepdims=True)
    return centred * lax.rsqrt(variance + 1e-05)


def attend_row(query_row, key_row, value_row, bias_block, key_keep, head_count):
    query_count = query_row.shape[0]
    key_count = key_row.shape[0]
    head_size = query_row.shape[1] // head_count
    query_heads = query_row.reshape(query_count, head_count, head_size)
    key_heads = key_row.reshape(key_count, head_count, head_size)
    value_heads = value_row.reshape(key_count, head_count, head_size)
    scores = jnp.einsum("jhd,khd->hjk", query_heads, key_heads, precision=HIGHEST) + bias_block
    scores = jnp.where(key_keep[None, None, :], scores, MASKED)
    weights = jnp.exp(scores)
    totals = jnp.sum(weights, axis=2)
    mixed = (
        jnp.einsum("hjk,khd->jhd", weights, value_heads, precision=HIGHEST)
        / jnp.transpose(totals)[:, :, None]
    )
    return mixed.reshape(query_count, head_count * head_size)


def project_all(normed, projection, head_count):
    stacked = jnp.einsum("rnc,pcd->prnd", normed, projection, precision=HIGHEST)
    q_scale = (normed.shape[2] // head_count) ** (-0.5)
    return (stacked[0] * q_scale, stacked[1], stacked[2], jax.nn.sigmoid(stacked[3]))


def make_update(queries, key_rows, value_rows, gate_rows, out_weight, key_keep, head_count):

    def update(bias_block, offset):

        def one_row(inputs):
            return attend_row(inputs[0], inputs[1], inputs[2], bias_block, key_keep, head_count)

        mixed = lax.map(one_row, (queries, key_rows, value_rows))
        return jnp.einsum("rjc,cd->rjd", mixed * gate_rows, out_weight, precision=HIGHEST)

    return update


def per_device(
    pair_rows, valid_count, start_proj, start_out, start_bias, end_proj, end_out, end_bias
):
    head_count = start_bias.shape[1]
    length = pair_rows.shape[1]
    key_keep = lax.iota(jnp.int32, length) < valid_count[0]
    normed = layer_norm(pair_rows)
    queries, key_rows, value_rows, gate_rows = project_all(normed, start_proj, head_count)
    local_bias = jnp.einsum("rkc,ch->hrk", normed, start_bias, precision=HIGHEST)
    start_update = make_update(
        queries, key_rows, value_rows, gate_rows, start_out, key_keep, head_count
    )
    updated = pair_rows + start_update(
        lax.all_gather(local_bias, ("row", "col"), axis=1, tiled=True), jnp.int32(0)
    )
    columns = lax.all_to_all(updated, ("row", "col"), split_axis=1, concat_axis=0, tiled=True)
    turned = jnp.swapaxes(columns, 0, 1)
    normed_turned = layer_norm(turned)
    queries_t, key_rows_t, value_rows_t, gate_rows_t = project_all(
        normed_turned, end_proj, head_count
    )
    local_turned = jnp.einsum("rkc,ch->hrk", normed_turned, end_bias, precision=HIGHEST)
    end_fn = make_update(
        queries_t, key_rows_t, value_rows_t, gate_rows_t, end_out, key_keep, head_count
    )
    end_update = end_fn(
        lax.all_gather(local_turned, ("row", "col"), axis=1, tiled=True), jnp.int32(0)
    )
    return turned + end_update


def solution(mesh):
    return jax.shard_map(
        per_device,
        mesh=mesh,
        in_specs=(P(("row", "col"), None, None), P(), P(), P(), P(), P(), P(), P()),
        out_specs=P(("row", "col"), None, None),
        check_vma=False,
    )
```

profile of v0, /device:TPU:1, one launch (start us, length us, event | category | flops | bytes accessed | tf_op | source)
XLA Modules:
  0.0 574.7 jit_solution(15946470037584841497)
XLA Ops:
  6.5 2.5 reduce_sum.54
  9.1 1.4 multiply_reduce_fusion.1
  10.5 3.9 fusion.51
  14.6 7.8 %convolution_bitcast_fusion.3 = f32[4,6,768,128]{3,2,0,1:T(8,128)S(1)} fusion(f32[6,768,128]{2,1,0:T(8,128)S(1)} %copy-done.2, f32[6,768]{1,0:T(8,128)S(1)} %add_rsqrt_fusion.1, f32[6,768]{1,0:T(8,128)S(1)} %broadcast_multiply_fusion.1, f32[4,128,128]{2,1,0:T(8,128)S(1)} %copy-done), kind=kOutput, calls=%fused_computation.19 | convolution fusion | flops 3625058304 | bytes 12095488 | tf_op jit(solution)/shard_map/rnc,pcd->prnd/dot_general | solution.py:36
  22.4 3.6 copy-done.4
  26.0 2.9 slice_bitcast_fusion.2
  28.9 60.3 %all-gather.3.cloned.1.call-done = f32[4,768,768]{2,0,1:T(4,128)} async-done(((f32[4,6,768]{2,0,1:T(4,128)}), f32[4,768,768]{2,0,1:T(4,128)}) %all-gather.3.cloned.1.call-update) | async-done | bytes 9437200 | tf_op jit(solution)/shard_map/all_gather | solution.py:67
  89.2 12.4 %copy.36 = f32[4,768,768]{1,2,0:T(8,128)} copy(f32[4,768,768]{2,0,1:T(4,128)} %all-gather.3.cloned.1.call-done) | data formatting | bytes 18874368
  101.6 1.6 broadcast.62.clone2
  103.1 156.2 %while.22 = (s32[]{:T(128)}, f32[6,768,128]{2,1,0:T(8,128)}, f32[6,768,128]{2,1,0:T(8,128)}, f32[6,768,128]{2,1,0:T(8,128)}, f32[6,768,128]{2,1,0:T(8,128)S(1)},...) while((s32[]{:T(128)}, f32[6,768,128]{2,1,0:T(8,128)}, f32[6,768,128]{2,1,0:T(8,128)}, ...), condition=%wide.region_4.5_spmd.clone, body=%wide.region_2.4_spmd.clone.sunk | while | flops 1819113216 | bytes 55077016 | solution.py:48
  103.1 1.4 constant_dynamic-slice_fusion.11
  105.5 13.4 %fusion.88 = (f32[4,768]{1,0:T(4,128)S(1)}, f32[4,768,768]{1,2,0:T(8,128)}) fusion(f32[4,768,768]{1,2,0:T(8,128)} %get-tuple-element.322, f32[768,4,32]{0,2,1:T(8,128)S(1)} %bitcast.153, f32[768,4,32]{0,2,1:T(8,128)S(1)} %bitcast.155, pred[768]{0:T(1024)(128)(4,1)S(1)} %iota_compare_fusion.4), kind=kOutput, calls=%fused_computation.81.clone.1 | convolution fusion | flops 913044480 | bytes 19673856 | tf_op jit(solution)/shard_map/while/body/eval_jaxpr/jhd,khd->hjk/dot_general | solution.py:24
  118.9 1.0 constant_dynamic-slice_fusion.10
  120.1 8.1 %fusion.89 = f32[768,4,32]{0,2,1:T(8,128)S(1)} fusion(f32[768,4,32]{0,2,1:T(8,128)S(1)} %bitcast.149, f32[4,768,768]{1,2,0:T(8,128)} %get-tuple-element.288, f32[768,4]{0,1:T(4,128)S(1)} %bitcast.158), kind=kOutput, calls=%fused_computation.4.clone.1 | convolution fusion | flops 906067968 | bytes 10235904 | tf_op jit(solution)/shard_map/while/body/eval_jaxpr/hjk,khd->jhd/dot_general | solution.py:29
  129.2 1.3 constant_dynamic-slice_fusion.11
  131.5 13.4 %fusion.88 = (f32[4,768]{1,0:T(4,128)S(1)}, f32[4,768,768]{1,2,0:T(8,128)}) fusion(f32[4,768,768]{1,2,0:T(8,128)} %get-tuple-element.322, f32[768,4,32]{0,2,1:T(8,128)S(1)} %bitcast.153, f32[768,4,32]{0,2,1:T(8,128)S(1)} %bitcast.155, pred[768]{0:T(1024)(128)(4,1)S(1)} %iota_compare_fusion.4), kind=kOutput, calls=%fused_computation.81.clone.1 | convolution fusion | flops 913044480 | bytes 19673856 | tf_op jit(solution)/shard_map/while/body/eval_jaxpr/jhd,khd->hjk/dot_general | solution.py:24
  144.9 1.0 constant_dynamic-slice_fusion.10
  146.1 8.1 %fusion.89 = f32[768,4,32]{0,2,1:T(8,128)S(1)} fusion(f32[768,4,32]{0,2,1:T(8,128)S(1)} %bitcast.149, f32[4,768,768]{1,2,0:T(8,128)} %get-tuple-element.288, f32[768,4]{0,1:T(4,128)S(1)} %bitcast.158), kind=kOutput, calls=%fused_computation.4.clone.1 | convolution fusion | flops 906067968 | bytes 10235904 | tf_op jit(solution)/shard_map/while/body/eval_jaxpr/hjk,khd->jhd/dot_general | solution.py:29
  155.2 1.3 constant_dynamic-slice_fusion.11
  157.6 13.4 %fusion.88 = (f32[4,768]{1,0:T(4,128)S(1)}, f32[4,768,768]{1,2,0:T(8,128)}) fusion(f32[4,768,768]{1,2,0:T(8,128)} %get-tuple-element.322, f32[768,4,32]{0,2,1:T(8,128)S(1)} %bitcast.153, f32[768,4,32]{0,2,1:T(8,128)S(1)} %bitcast.155, pred[768]{0:T(1024)(128)(4,1)S(1)} %iota_compare_fusion.4), kind=kOutput, calls=%fused_computation.81.clone.1 | convolution fusion | flops 913044480 | bytes 19673856 | tf_op jit(solution)/shard_map/while/body/eval_jaxpr/jhd,khd->hjk/dot_general | solution.py:24
  171.0 1.0 constant_dynamic-slice_fusion.10
  172.2 8.1 %fusion.89 = f32[768,4,32]{0,2,1:T(8,128)S(1)} fusion(f32[768,4,32]{0,2,1:T(8,128)S(1)} %bitcast.149, f32[4,768,768]{1,2,0:T(8,128)} %get-tuple-element.288, f32[768,4]{0,1:T(4,128)S(1)} %bitcast.158), kind=kOutput, calls=%fused_computation.4.clone.1 | convolution fusion | flops 906067968 | bytes 10235904 | tf_op jit(solution)/shard_map/while/body/eval_jaxpr/hjk,khd->jhd/dot_general | solution.py:29
  181.2 1.3 constant_dynamic-slice_fusion.11
  183.6 13.4 %fusion.88 = (f32[4,768]{1,0:T(4,128)S(1)}, f32[4,768,768]{1,2,0:T(8,128)}) fusion(f32[4,768,768]{1,2,0:T(8,128)} %get-tuple-element.322, f32[768,4,32]{0,2,1:T(8,128)S(1)} %bitcast.153, f32[768,4,32]{0,2,1:T(8,128)S(1)} %bitcast.155, pred[768]{0:T(1024)(128)(4,1)S(1)} %iota_compare_fusion.4), kind=kOutput, calls=%fused_computation.81.clone.1 | convolution fusion | flops 913044480 | bytes 19673856 | tf_op jit(solution)/shard_map/while/body/eval_jaxpr/jhd,khd->hjk/dot_general | solution.py:24
  198.2 8.1 %fusion.89 = f32[768,4,32]{0,2,1:T(8,128)S(1)} fusion(f32[768,4,32]{0,2,1:T(8,128)S(1)} %bitcast.149, f32[4,768,768]{1,2,0:T(8,128)} %get-tuple-element.288, f32[768,4]{0,1:T(4,128)S(1)} %bitcast.158), kind=kOutput, calls=%fused_computation.4.clone.1 | convolution fusion | flops 906067968 | bytes 10235904 | tf_op jit(solution)/shard_map/while/body/eval_jaxpr/hjk,khd->jhd/dot_general | solution.py:29
  207.2 1.3 constant_dynamic-slice_fusion.11
  209.6 13.4 %fusion.88 = (f32[4,768]{1,0:T(4,128)S(1)}, f32[4,768,768]{1,2,0:T(8,128)}) fusion(f32[4,768,768]{1,2,0:T(8,128)} %get-tuple-element.322, f32[768,4,32]{0,2,1:T(8,128)S(1)} %bitcast.153, f32[768,4,32]{0,2,1:T(8,128)S(1)} %bitcast.155, pred[768]{0:T(1024)(128)(4,1)S(1)} %iota_compare_fusion.4), kind=kOutput, calls=%fused_computation.81.clone.1 | convolution fusion | flops 913044480 | bytes 19673856 | tf_op jit(solution)/shard_map/while/body/eval_jaxpr/jhd,khd->hjk/dot_general | solution.py:24
  224.2 8.1 %fusion.89 = f32[768,4,32]{0,2,1:T(8,128)S(1)} fusion(f32[768,4,32]{0,2,1:T(8,128)S(1)} %bitcast.149, f32[4,768,768]{1,2,0:T(8,128)} %get-tuple-element.288, f32[768,4]{0,1:T(4,128)S(1)} %bitcast.158), kind=kOutput, calls=%fused_computation.4.clone.1 | convolution fusion | flops 906067968 | bytes 10235904 | tf_op jit(solution)/shard_map/while/body/eval_jaxpr/hjk,khd->jhd/dot_general | solution.py:29
  233.3 1.3 constant_dynamic-slice_fusion.11
  235.6 13.4 %fusion.88 = (f32[4,768]{1,0:T(4,128)S(1)}, f32[4,768,768]{1,2,0:T(8,128)}) fusion(f32[4,768,768]{1,2,0:T(8,128)} %get-tuple-element.322, f32[768,4,32]{0,2,1:T(8,128)S(1)} %bitcast.153, f32[768,4,32]{0,2,1:T(8,128)S(1)} %bitcast.155, pred[768]{0:T(1024)(128)(4,1)S(1)} %iota_compare_fusion.4), kind=kOutput, calls=%fused_computation.81.clone.1 | convolution fusion | flops 913044480 | bytes 19673856 | tf_op jit(solution)/shard_map/while/body/eval_jaxpr/jhd,khd->hjk/dot_general | solution.py:24
  250.3 8.1 %fusion.89 = f32[768,4,32]{0,2,1:T(8,128)S(1)} fusion(f32[768,4,32]{0,2,1:T(8,128)S(1)} %bitcast.149, f32[4,768,768]{1,2,0:T(8,128)} %get-tuple-element.288, f32[768,4]{0,1:T(4,128)S(1)} %bitcast.158), kind=kOutput, calls=%fused_computation.4.clone.1 | convolution fusion | flops 906067968 | bytes 10235904 | tf_op jit(solution)/shard_map/while/body/eval_jaxpr/hjk,khd->jhd/dot_general | solution.py:29
  259.3 5.5 fusion.35
  264.8 1.4 copy.38
  266.2 47.0 %all_to_all.18 = f32[6,768,128]{2,0,1:T(8,128)S(1)} all-to-all(f32[6,768,128]{2,0,1:T(8,128)S(1)} %copy.38), channel_id=1, replica_groups=mesh['row'=8,'col'=16] {'row','col'}, dimensions={1} | all-to-all | bytes 4718592 | tf_op jit(solution)/shard_map/all_to_all | solution.py:69
  313.3 1.8 copy.40
  315.1 2.6 all_to_all.16
  318.5 1.4 multiply_reduce_fusion
  319.9 3.9 fusion.48
  323.9 7.8 %convolution_bitcast_fusion.2 = f32[4,6,768,128]{3,2,0,1:T(8,128)S(1)} fusion(f32[768,6,128]{2,0,1:T(8,128)S(1)} %all_to_all.16, f32[6,768]{1,0:T(8,128)S(1)} %add_rsqrt_fusion, f32[6,768]{1,0:T(8,128)S(1)} %broadcast_multiply_fusion, f32[4,128,128]{2,1,0:T(8,128)S(1)} %copy-done.7), kind=kOutput, calls=%fused_computation.18 | convolution fusion | flops 3625058304 | bytes 12095488 | tf_op jit(solution)/shard_map/rnc,pcd->prnd/dot_general | solution.py:36
  331.7 3.6 copy-done.3
  335.4 3.2 slice_bitcast_fusion
  338.5 53.1 %all-gather.5.cloned.1.call-done = f32[4,768,768]{2,0,1:T(4,128)} async-done(((f32[4,6,768]{2,0,1:T(4,128)}), f32[4,768,768]{2,0,1:T(4,128)}) %all-gather.5.cloned.1.call-update) | async-done | bytes 9437200 | tf_op jit(solution)/shard_map/all_gather | solution.py:80
  391.6 11.9 %copy.44 = f32[4,768,768]{1,2,0:T(8,128)} copy(f32[4,768,768]{2,0,1:T(4,128)} %all-gather.5.cloned.1.call-done) | data formatting | bytes 18874368
  403.6 1.5 broadcast.62.clone
  405.1 156.4 %while.23 = (s32[]{:T(128)}, f32[6,768,128]{2,1,0:T(8,128)}, f32[6,768,128]{2,1,0:T(8,128)}, f32[6,768,128]{2,1,0:T(8,128)}, f32[6,768,128]{2,1,0:T(8,128)}, /*index=5*/f32[4,768,768]{1,2,0:T(8,128)}, s32[]{:T(128)}, s32[]{:T(128)}) while((s32[]{:T(128)}, f32[6,768,128]{2,1,0:T(8,128)}, f32[6,768,128]{2,1,0:T(8,128)}, ...), condition=%wide.region_9.10_spmd.clone, body=%wide.region_7.9_spmd.clone.sunk | while | flops 1819113216 | bytes 36202592 | solution.py:48
  405.3 1.2 constant_dynamic-slice_fusion.13
  408.2 13.0 %fusion.94 = (f32[4,768]{1,0:T(4,128)S(1)}, f32[4,768,768]{1,2,0:T(8,128)}) fusion(f32[4,768,768]{1,2,0:T(8,128)} %get-tuple-element.346, f32[768,4,32]{0,2,1:T(8,128)} %bitcast.154, f32[768,4,32]{0,2,1:T(8,128)S(1)} %bitcast.156, pred[768]{0:T(1024)(128)(4,1)S(1)} %iota_compare_fusion.5), kind=kOutput, calls=%fused_computation.82.clone.1 | convolution fusion | flops 913044480 | bytes 19673856 | tf_op jit(solution)/shard_map/while/body/eval_jaxpr/jhd,khd->hjk/dot_general | solution.py:24
  422.5 7.9 %fusion.95 = f32[768,4,32]{0,2,1:T(8,128)S(1)} fusion(f32[768,4,32]{0,2,1:T(8,128)S(1)} %bitcast.151, f32[4,768,768]{1,2,0:T(8,128)} %get-tuple-element.299, f32[768,4]{0,1:T(4,128)S(1)} %bitcast.159), kind=kOutput, calls=%fused_computation.12.clone.1 | convolution fusion | flops 906067968 | bytes 10235904 | tf_op jit(solution)/shard_map/while/body/eval_jaxpr/hjk,khd->jhd/dot_general | solution.py:29
  431.4 1.2 constant_dynamic-slice_fusion.13
  434.3 13.0 %fusion.94 = (f32[4,768]{1,0:T(4,128)S(1)}, f32[4,768,768]{1,2,0:T(8,128)}) fusion(f32[4,768,768]{1,2,0:T(8,128)} %get-tuple-element.346, f32[768,4,32]{0,2,1:T(8,128)} %bitcast.154, f32[768,4,32]{0,2,1:T(8,128)S(1)} %bitcast.156, pred[768]{0:T(1024)(128)(4,1)S(1)} %iota_compare_fusion.5), kind=kOutput, calls=%fused_computation.82.clone.1 | convolution fusion | flops 913044480 | bytes 19673856 | tf_op jit(solution)/shard_map/while/body/eval_jaxpr/jhd,khd->hjk/dot_general | solution.py:24
  448.5 7.9 %fusion.95 = f32[768,4,32]{0,2,1:T(8,128)S(1)} fusion(f32[768,4,32]{0,2,1:T(8,128)S(1)} %bitcast.151, f32[4,768,768]{1,2,0:T(8,128)} %get-tuple-element.299, f32[768,4]{0,1:T(4,128)S(1)} %bitcast.159), kind=kOutput, calls=%fused_computation.12.clone.1 | convolution fusion | flops 906067968 | bytes 10235904 | tf_op jit(solution)/shard_map/while/body/eval_jaxpr/hjk,khd->jhd/dot_general | solution.py:29
  457.4 1.2 constant_dynamic-slice_fusion.13
  460.3 13.0 %fusion.94 = (f32[4,768]{1,0:T(4,128)S(1)}, f32[4,768,768]{1,2,0:T(8,128)}) fusion(f32[4,768,768]{1,2,0:T(8,128)} %get-tuple-element.346, f32[768,4,32]{0,2,1:T(8,128)} %bitcast.154, f32[768,4,32]{0,2,1:T(8,128)S(1)} %bitcast.156, pred[768]{0:T(1024)(128)(4,1)S(1)} %iota_compare_fusion.5), kind=kOutput, calls=%fused_computation.82.clone.1 | convolution fusion | flops 913044480 | bytes 19673856 | tf_op jit(solution)/shard_map/while/body/eval_jaxpr/jhd,khd->hjk/dot_general | solution.py:24
  474.5 7.9 %fusion.95 = f32[768,4,32]{0,2,1:T(8,128)S(1)} fusion(f32[768,4,32]{0,2,1:T(8,128)S(1)} %bitcast.151, f32[4,768,768]{1,2,0:T(8,128)} %get-tuple-element.299, f32[768,4]{0,1:T(4,128)S(1)} %bitcast.159), kind=kOutput, calls=%fused_computation.12.clone.1 | convolution fusion | flops 906067968 | bytes 10235904 | tf_op jit(solution)/shard_map/while/body/eval_jaxpr/hjk,khd->jhd/dot_general | solution.py:29
  483.4 1.2 constant_dynamic-slice_fusion.13
  486.3 13.0 %fusion.94 = (f32[4,768]{1,0:T(4,128)S(1)}, f32[4,768,768]{1,2,0:T(8,128)}) fusion(f32[4,768,768]{1,2,0:T(8,128)} %get-tuple-element.346, f32[768,4,32]{0,2,1:T(8,128)} %bitcast.154, f32[768,4,32]{0,2,1:T(8,128)S(1)} %bitcast.156, pred[768]{0:T(1024)(128)(4,1)S(1)} %iota_compare_fusion.5), kind=kOutput, calls=%fused_computation.82.clone.1 | convolution fusion | flops 913044480 | bytes 19673856 | tf_op jit(solution)/shard_map/while/body/eval_jaxpr/jhd,khd->hjk/dot_general | solution.py:24
  500.6 7.9 %fusion.95 = f32[768,4,32]{0,2,1:T(8,128)S(1)} fusion(f32[768,4,32]{0,2,1:T(8,128)S(1)} %bitcast.151, f32[4,768,768]{1,2,0:T(8,128)} %get-tuple-element.299, f32[768,4]{0,1:T(4,128)S(1)} %bitcast.159), kind=kOutput, calls=%fused_computation.12.clone.1 | convolution fusion | flops 906067968 | bytes 10235904 | tf_op jit(solution)/shard_map/while/body/eval_jaxpr/hjk,khd->jhd/dot_general | solution.py:29
  509.5 1.2 constant_dynamic-slice_fusion.13
  512.4 13.0 %fusion.94 = (f32[4,768]{1,0:T(4,128)S(1)}, f32[4,768,768]{1,2,0:T(8,128)}) fusion(f32[4,768,768]{1,2,0:T(8,128)} %get-tuple-element.346, f32[768,4,32]{0,2,1:T(8,128)} %bitcast.154, f32[768,4,32]{0,2,1:T(8,128)S(1)} %bitcast.156, pred[768]{0:T(1024)(128)(4,1)S(1)} %iota_compare_fusion.5), kind=kOutput, calls=%fused_computation.82.clone.1 | convolution fusion | flops 913044480 | bytes 19673856 | tf_op jit(solution)/shard_map/while/body/eval_jaxpr/jhd,khd->hjk/dot_general | solution.py:24
  526.6 7.9 %fusion.95 = f32[768,4,32]{0,2,1:T(8,128)S(1)} fusion(f32[768,4,32]{0,2,1:T(8,128)S(1)} %bitcast.151, f32[4,768,768]{1,2,0:T(8,128)} %get-tuple-element.299, f32[768,4]{0,1:T(4,128)S(1)} %bitcast.159), kind=kOutput, calls=%fused_computation.12.clone.1 | convolution fusion | flops 906067968 | bytes 10235904 | tf_op jit(solution)/shard_map/while/body/eval_jaxpr/hjk,khd->jhd/dot_general | solution.py:29
  535.5 1.2 constant_dynamic-slice_fusion.13
  538.5 13.0 %fusion.94 = (f32[4,768]{1,0:T(4,128)S(1)}, f32[4,768,768]{1,2,0:T(8,128)}) fusion(f32[4,768,768]{1,2,0:T(8,128)} %get-tuple-element.346, f32[768,4,32]{0,2,1:T(8,128)} %bitcast.154, f32[768,4,32]{0,2,1:T(8,128)S(1)} %bitcast.156, pred[768]{0:T(1024)(128)(4,1)S(1)} %iota_compare_fusion.5), kind=kOutput, calls=%fused_computation.82.clone.1 | convolution fusion | flops 913044480 | bytes 19673856 | tf_op jit(solution)/shard_map/while/body/eval_jaxpr/jhd,khd->hjk/dot_general | solution.py:24
  552.7 7.9 %fusion.95 = f32[768,4,32]{0,2,1:T(8,128)S(1)} fusion(f32[768,4,32]{0,2,1:T(8,128)S(1)} %bitcast.151, f32[4,768,768]{1,2,0:T(8,128)} %get-tuple-element.299, f32[768,4]{0,1:T(4,128)S(1)} %bitcast.159), kind=kOutput, calls=%fused_computation.12.clone.1 | convolution fusion | flops 906067968 | bytes 10235904 | tf_op jit(solution)/shard_map/while/body/eval_jaxpr/hjk,khd->jhd/dot_general | solution.py:29
  561.6 6.1 %bitcast_add_fusion = f32[6,768,128]{2,1,0:T(8,128)} fusion(f32[768,6,128]{2,0,1:T(8,128)S(1)} %all_to_all.16, f32[6,768,128]{2,1,0:T(8,128)} %get-tuple-element.80, f32[4,6,768,128]{3,2,0,1:T(8,128)} %copy-done.3, f32[128,128]{1,0:T(8,128)S(1)} %copy-done.11), kind=kOutput, calls=%fused_computation.42 | convolution fusion | flops 908918784 | bytes 9502720 | tf_op jit(solution)/shard_map/rjc,cd->rjd/dot_general | solution.py:49
  (132 shorter events, 39.8 us)
Async XLA Ops:
  6.5 8.0 %copy-start = (f32[4,128,128]{2,1,0:T(8,128)S(1)}, f32[4,128,128]{2,1,0:T(8,128)}, u32[]{:S(2)}) copy-start(f32[4,128,128]{2,1,0:T(8,128)} %param.14) | copy-start | bytes 786436
  6.5 2.5 copy-start.2
  6.5 4.0 copy-start.8
  6.5 82.6 %all-gather.3.cloned.1.call-start = ((), (), s32[]{:S(2)}) async-start(), calls=%async_computation.1 | async-start | bytes 9510912 | tf_op jit(solution)/shard_map/all_gather | solution.py:67
  14.5 377.1 %all-gather.5.cloned.1.call-start = ((), (), s32[]{:S(2)}) async-start(), calls=%async_computation.2 | async-start | bytes 9510912 | tf_op jit(solution)/shard_map/all_gather | solution.py:80
  22.4 3.6 copy-start.4
  103.1 156.2 %copy-start.10 = (f32[128,128]{1,0:T(8,128)S(1)}, f32[128,128]{1,0:T(8,128)}, u32[]{:S(2)}) copy-start(f32[128,128]{1,0:T(8,128)} %param.15) | copy-start | bytes 196612
  103.1 1.4 copy-start.5
  120.1 9.1 %copy-start.6 = (f32[6,768,128]{2,1,0:T(8,128)S(1)}, f32[6,768,128]{2,1,0:T(8,128)}, u32[]{:S(2)}) copy-start(f32[6,768,128]{2,1,0:T(8,128)} %copy-done.5) | copy-start | bytes 7077892 | tf_op jit(solution)/shard_map/while
  129.2 1.4 copy-start.5
  146.1 9.1 %copy-start.6 = (f32[6,768,128]{2,1,0:T(8,128)S(1)}, f32[6,768,128]{2,1,0:T(8,128)}, u32[]{:S(2)}) copy-start(f32[6,768,128]{2,1,0:T(8,128)} %copy-done.5) | copy-start | bytes 7077892 | tf_op jit(solution)/shard_map/while
  155.2 1.4 copy-start.5
  172.2 9.1 %copy-start.6 = (f32[6,768,128]{2,1,0:T(8,128)S(1)}, f32[6,768,128]{2,1,0:T(8,128)}, u32[]{:S(2)}) copy-start(f32[6,768,128]{2,1,0:T(8,128)} %copy-done.5) | copy-start | bytes 7077892 | tf_op jit(solution)/shard_map/while
  181.2 1.4 copy-start.5
  198.2 9.1 %copy-start.6 = (f32[6,768,128]{2,1,0:T(8,128)S(1)}, f32[6,768,128]{2,1,0:T(8,128)}, u32[]{:S(2)}) copy-start(f32[6,768,128]{2,1,0:T(8,128)} %copy-done.5) | copy-start | bytes 7077892 | tf_op jit(solution)/shard_map/while
  207.2 1.4 copy-start.5
  224.2 9.1 %copy-start.6 = (f32[6,768,128]{2,1,0:T(8,128)S(1)}, f32[6,768,128]{2,1,0:T(8,128)}, u32[]{:S(2)}) copy-start(f32[6,768,128]{2,1,0:T(8,128)} %copy-done.5) | copy-start | bytes 7077892 | tf_op jit(solution)/shard_map/while
  233.3 1.4 copy-start.5
  250.2 9.1 %copy-start.6 = (f32[6,768,128]{2,1,0:T(8,128)S(1)}, f32[6,768,128]{2,1,0:T(8,128)}, u32[]{:S(2)}) copy-start(f32[6,768,128]{2,1,0:T(8,128)} %copy-done.5) | copy-start | bytes 7077892 | tf_op jit(solution)/shard_map/while
  317.8 2.2 copy-start.9
  318.5 5.4 copy-start.7
  331.7 3.6 copy-start.3
  405.1 156.5 %copy-start.11 = (f32[128,128]{1,0:T(8,128)S(1)}, f32[128,128]{1,0:T(8,128)}, u32[]{:S(2)}) copy-start(f32[128,128]{1,0:T(8,128)} %param.18) | copy-start | bytes 196612
  561.6 6.1 %copy-start.1 = (f32[4,128,128]{2,1,0:T(8,128)S(1)}, f32[4,128,128]{2,1,0:T(8,128)}, u32[]{:S(2)}) copy-start(f32[4,128,128]{2,1,0:T(8,128)} %param.14) | copy-start | bytes 786436
Sparse Core Ops, SparseCore 0:
  14.6 74.5 all-gather.2
  324.0 67.5 all-gather.4
where the time goes:
time: 584 us; the launch traced here: 575 us
  matrix products  290 us (50%)
  waiting for transfers between devices  113 us (19%)
  local copies, waits for them, and re-layouts  89.7 us (15%)
  blocking collectives  47 us (8%)
  other arithmetic  19.9 us (3%)
  between operations  13.8 us (2%)
    dot_general x12, matrix products, attend_row(): jnp.einsum('jhd,khd->hjk', query_heads, key_heads, precision=HIGHEST)  159 us
    dot_general x12, matrix products, attend_row(): jnp.einsum('hjk,khd->jhd', weights, value_heads, precision=HIGHEST)  96.2 us
    all_gather x1, waiting for transfers between devices, per_device(): lax.all_gather(local_bias, ('row', 'col'), axis=1, tiled=True)  60.3 us
    all_gather x1, waiting for transfers between devices, per_device(): lax.all_gather(local_turned, ('row', 'col'), axis=1, tiled=True)  53.1 us
    all_to_all x1, blocking collectives, per_device(): lax.all_to_all(updated, ('row', 'col'), split_axis=1, concat_axis=0, tile...  47 us
    dynamic_slice x60, local copies, waits for them, and re-layouts, update(): mixed = lax.map(one_row, (queries, key_rows, value_rows))  37.5 us
    unnamed x22, local copies, waits for them, and re-layouts  31.6 us
    dot_general x2, matrix products, project_all(): stacked = jnp.einsum('rnc,pcd->prnd', normed, projection, precision=HIGHEST)  15.6 us
  transfers between devices with their start and end apart: 2, of which 2 were waited for; matrix products, arithmetic and copies ran while one was open for 4% of the time, Pallas kernels for 0%

commit v1 on v0

v1 whole, which is shorter than its diff:
```python
import functools
import jax
import jax.numpy as jnp
from jax import lax
from jax.sharding import PartitionSpec as P
from jax.experimental import pallas as pl
from jax.experimental.pallas import tpu as pltpu

LOG2E = 1.4426950408889634
BF = jnp.bfloat16
F32 = jnp.float32
HIGHEST = lax.Precision.HIGHEST
ROWS, N, C, H, D = 6, 768, 128, 4, 32


def normalise(values):
    average = jnp.mean(values, axis=-1, keepdims=True)
    centred = values - average
    variance = jnp.mean(centred * centred, axis=-1, keepdims=True)
    return centred * lax.rsqrt(variance + 1e-05)


def halves(values):
    high = values.astype(BF)
    return high, (values - high.astype(F32)).astype(BF)


def bias_kernel(z_ref, weight_ref, bias_ref):
    u = normalise(z_ref[0])
    b = lax.dot_general(
        weight_ref[...], u, (((1,), (1,)), ((), ())), precision=HIGHEST, preferred_element_type=F32
    )
    for block in range(N // 128):
        bias_ref[0, block * H : (block + 1) * H, :] = b[:H, block * 128 : (block + 1) * 128]


def bias_call(z, bias_weight):
    rows = z.shape[0]
    weight = jnp.pad(bias_weight.T * LOG2E, ((0, 8 - H), (0, 0)))
    return pl.pallas_call(
        bias_kernel,
        grid=(rows,),
        in_specs=[
            pl.BlockSpec((1, N, C), lambda r: (r, 0, 0)),
            pl.BlockSpec((8, C), lambda r: (0, 0)),
        ],
        out_specs=pl.BlockSpec((1, N // 128 * H, 128), lambda r: (r, 0, 0)),
        out_shape=jax.ShapeDtypeStruct((rows, N // 128 * H, 128), F32),
        cost_estimate=pl.CostEstimate(flops=rows * N * C * 20, bytes_accessed=rows * N * C * 4, transcendentals=0),
        name="bias",
    )(z, weight)


def project_kernel(valid_ref, z_ref, p_ref, q_ref, k_ref, v_ref, g_ref, w_ref, wg_ref):
    lane = lax.broadcasted_iota(jnp.int32, (1, C), 1)
    group = lane // D

    @pl.when(pl.program_id(0) == 0)
    def _():
        group_c = lax.broadcasted_iota(jnp.int32, (C, C), 1) // D
        for part in range(3):
            base = p_ref[part]
            if part == 0:
                base = base * (LOG2E * D**-0.5)
            turned = [base] + [pltpu.roll(base, D * m, 1) for m in range(1, 4)]
            for head in range(H):
                block = turned[(0 - head) % H]
                for g in range(1, H):
                    block = jnp.where(group_c == g, turned[(g - head) % H], block)
                high, low = halves(block)
                at = pl.ds((part * H + head) * C, C)
                w_ref[0, :C, at] = high
                w_ref[0, C:, at] = high
                w_ref[1, :C, at] = low
                w_ref[1, C:, at] = low
        high, low = halves(p_ref[3])
        wg_ref[0, :C] = high
        wg_ref[0, C:] = high
        wg_ref[1, :C] = low
        wg_ref[1, C:] = low

    u = normalise(z_ref[0])
    u_high, u_low = halves(u)
    u2 = jnp.concatenate([u_high, u_low], axis=1)

    def project(w):
        return jnp.dot(u2, w[0], preferred_element_type=F32) + jnp.dot(
            u2, w[1], preferred_element_type=F32
        )

    dead = lax.broadcasted_iota(jnp.int32, (N, 1), 0) >= valid_ref[0]
    dead_value = jnp.where(dead, -1e9, 0.0)
    for part in range(3):
        for head in range(H):
            at = pl.ds((part * H + head) * C, C)
            x = project((w_ref[0, :, at], w_ref[1, :, at]))
            high = x.astype(BF).astype(F32)
            low = x - high
            if part == 0:
                out = jnp.where(group == 1, low, high)
                out = jnp.where(group == 3, jnp.where(lane == 3 * D, 1.0, 0.0), out)
                q_ref[0, head] = out.astype(BF)
            elif part == 1:
                out = jnp.where(group == 2, low, high)
                out = jnp.where(group == 3, jnp.where(lane == 3 * D, dead_value, 0.0), out)
                k_ref[0, head] = out.astype(BF)
            else:
                out = jnp.where(group == (head + 1) % H, low, high)
                out = jnp.where(group == (head + 2) % H, 1.0, out)
                out = jnp.where(group == (head + 3) % H, 0.0, out)
                v_ref[0, head] = out.astype(BF)
    g_ref[0] = jax.nn.sigmoid(project((wg_ref[0], wg_ref[1])))


def project_call(z, projection, valid_count):
    rows = z.shape[0]
    heads = jax.ShapeDtypeStruct((rows, H, N, C), BF)
    head_spec = pl.BlockSpec((1, H, N, C), lambda r, s: (r, 0, 0, 0))
    row_spec = pl.BlockSpec((1, N, C), lambda r, s: (r, 0, 0))
    return pl.pallas_call(
        project_kernel,
        grid_spec=pltpu.PrefetchScalarGridSpec(
            num_scalar_prefetch=1,
            grid=(rows,),
            in_specs=[row_spec, pl.BlockSpec((4, C, C), lambda r, s: (0, 0, 0))],
            out_specs=[head_spec, head_spec, head_spec, row_spec],
            scratch_shapes=[
                pltpu.VMEM((2, 2 * C, 3 * H * C), BF),
                pltpu.VMEM((2, 2 * C, C), BF),
            ],
        ),
        out_shape=[heads, heads, heads, jax.ShapeDtypeStruct((rows, N, C), F32)],
        compiler_params=pltpu.CompilerParams(vmem_limit_bytes=50 * 2**20),
        cost_estimate=pl.CostEstimate(
            flops=rows * N * 2 * C * 2 * 13 * C * 2, bytes_accessed=rows * N * C * 4 * 8, transcendentals=0
        ),
        name="project",
    )(valid_count, z, projection)


def attend_kernel(QC, KT, valid_ref, q_ref, k_ref, v_ref, g_ref, z_ref, bias_ref, o_ref, out_ref,
                  bias_s, acc_s, o_s):
    lane = lax.broadcasted_iota(jnp.int32, (1, C), 1)
    group = lane // D

    @pl.when((pl.program_id(0) == 0) & (pl.program_id(1) == 0))
    def _():
        high, low = halves(o_ref[...])
        o_s[0, :C] = high
        o_s[0, C:] = high
        o_s[1, :C] = low
        o_s[1, C:] = low

    @pl.when(pl.program_id(1) == 0)
    def _():
        for block in range(N // 128):
            for head in range(H):
                bias_s[head, :, block * 128 : (block + 1) * 128] = bias_ref[
                    pl.ds(block * H + head, QC, stride=N // 128 * H), :
                ]

    def run(keys):
        for head in range(H):
            q = q_ref[0, head]
            acc = None
            for at in range(0, keys, KT):
                size = min(KT, keys - at)
                s = lax.dot_general(
                    q, k_ref[0, head, at : at + size, :], (((1,), (1,)), ((), ())),
                    preferred_element_type=F32,
                )
                w = jnp.exp2(s + bias_s[head, :, at : at + size])
                high, low = halves(w)
                v = v_ref[0, head, at : at + size, :]
                term = jnp.dot(high, v, preferred_element_type=F32) + jnp.dot(
                    low, v, preferred_element_type=F32
                )
                acc = term if acc is None else acc + term
            acc_s[head] = acc

    count = (valid_ref[0] + 127) // 128
    for blocks in range(3, N // 128 + 1):

        @pl.when(count == blocks)
        def _():
            run(blocks * 128)

    mixed = None
    for head in range(H):
        acc = acc_s[head]
        total = pltpu.roll(acc, 2 * D, 1)
        value = (acc + pltpu.roll(acc, 3 * D, 1)) / jnp.where(group == head, total, 1.0)
        mixed = value if mixed is None else jnp.where(group == head, value, mixed)
    high, low = halves(mixed * g_ref[0])
    both = jnp.concatenate([high, low], axis=1)
    out_ref[0] = (
        z_ref[0]
        + jnp.dot(both, o_s[0], preferred_element_type=F32)
        + jnp.dot(both, o_s[1], preferred_element_type=F32)
    )


def attend_call(q, k, v, g, z, bias, out_weight, valid_count, QC=256, KT=256):
    rows = z.shape[0]
    queries = z.shape[1]
    per = N // 128 * H
    key_spec = pl.BlockSpec((1, H, N, C), lambda c, r, s: (r, 0, 0, 0))
    row_spec = pl.BlockSpec((1, QC, C), lambda c, r, s: (r, c, 0))
    return pl.pallas_call(
        functools.partial(attend_kernel, QC, KT),
        grid_spec=pltpu.PrefetchScalarGridSpec(
            num_scalar_prefetch=1,
            grid=(queries // QC, rows),
            in_specs=[
                pl.BlockSpec((1, H, QC, C), lambda c, r, s: (r, 0, c, 0)),
                key_spec,
                key_spec,
                row_spec,
                row_spec,
                pl.BlockSpec((QC * per, 128), lambda c, r, s: (c, 0)),
                pl.BlockSpec((C, C), lambda c, r, s: (0, 0)),
            ],
            out_specs=row_spec,
            scratch_shapes=[
                pltpu.VMEM((H, QC, N), F32),
                pltpu.VMEM((H, QC, C), F32),
                pltpu.VMEM((2, 2 * C, C), BF),
            ],
        ),
        out_shape=jax.ShapeDtypeStruct(z.shape, F32),
        compiler_params=pltpu.CompilerParams(vmem_limit_bytes=50 * 2**20),
        cost_estimate=pl.CostEstimate(
            flops=rows * queries * N * H * 64 * 4, bytes_accessed=rows * N * C * 4 * 8, transcendentals=0
        ),
        name="attend",
    )(valid_count, q, k, v, g, z, bias, out_weight)


def per_device(
    pair_rows, valid_count, start_proj, start_out, start_bias, end_proj, end_out, end_bias
):
    axes = ("row", "col")

    def block(z, projection, out_weight, bias_weight):
        local = bias_call(z, bias_weight).reshape(-1, 128)
        bias = lax.all_gather(local, axes, axis=0, tiled=True)
        q, k, v, g = project_call(z, projection, valid_count)
        return attend_call(q, k, v, g, z, bias, out_weight, valid_count)

    updated = block(pair_rows, start_proj, start_out, start_bias)
    columns = lax.all_to_all(updated, axes, split_axis=1, concat_axis=0, tiled=True)
    turned = jnp.swapaxes(columns, 0, 1)
    return block(turned, end_proj, end_out, end_bias)


def solution(mesh):
    return jax.shard_map(
        per_device,
        mesh=mesh,
        in_specs=(P(("row", "col"), None, None), P(), P(), P(), P(), P(), P(), P()),
        out_specs=P(("row", "col"), None, None),
        check_vma=False,
    )
```

time: 584 us -> 352 us (0.60); the launches traced: 575 us -> 352 us
  matrix products: 290 us -> 0 us
  Pallas kernels: 0 us -> 181 us
  local copies, waits for them, and re-layouts: 89.7 us -> 12.6 us
  blocking collectives: 47 us -> 0 us
  waiting for transfers between devices: 113 us -> 137 us
  other arithmetic: 19.9 us -> 0.69 us
    dot_general x30 -> x0, matrix products: 290 us -> none  [the longest x12 159 us: attend_row(): jnp.einsum('jhd,khd->hjk', query_heads, key_heads, precision=HIGHEST)]
    pallas_call x0 -> x6, Pallas kernels: none -> 181 us  [the longest x2 126 us: attend_call(): pl.pallas_call(functools.partial(attend_kernel, QC, KT), grid_spec=pltpu....]
    all_to_all x1 -> x0, blocking collectives: 47 us -> none  [per_device(): lax.all_to_all(updated, ('row', 'col'), split_axis=1, concat_axis=0, tile...]
    all_to_all x0 -> x1, waiting for transfers between devices: none -> 41 us  [per_device(): lax.all_to_all(updated, axes, split_axis=1, concat_axis=0, tiled=True)]
    dynamic_slice x60 -> x0, local copies, waits for them, and re-layouts: 37.5 us -> none  [update(): mixed = lax.map(one_row, (queries, key_rows, value_rows))]
    unnamed x22 -> x12, local copies, waits for them, and re-layouts: 31.6 us -> 2.37 us
    all_gather x2, waiting for transfers between devices: 113 us -> 96.4 us  [block(): bias = lax.all_gather(local, axes, axis=0, tiled=True)]
    dynamic_update_slice x24 -> x0, local copies, waits for them, and re-layouts: 11.2 us -> none  [update(): mixed = lax.map(one_row, (queries, key_rows, value_rows))]
  transfers between devices with their start and end apart: 2 -> 3, of which waited for: 2 -> 3; matrix products, arithmetic and copies ran while one was open for 4% -> 0% of each run, Pallas kernels for 0% -> 12%
where the time goes in v1:
time: 352 us
  Pallas kernels  181 us (51%)
  waiting for transfers between devices  137 us (39%)
  between operations  14.1 us (4%)
  local copies, waits for them, and re-layouts  12.6 us (4%)
  starting transfers between devices  5.42 us (2%)
    pallas_call x2, Pallas kernels, attend_call(): pl.pallas_call(functools.partial(attend_kernel, QC, KT), grid_spec=pltpu....  126 us
    all_gather x2, waiting for transfers between devices, block(): bias = lax.all_gather(local, axes, axis=0, tiled=True)  96.4 us
    pallas_call x2, Pallas kernels, project_call(): pl.pallas_call(project_kernel, grid_spec=pltpu.PrefetchScalarGridSpec(num...  43 us
    all_to_all x1, waiting for transfers between devices, per_device(): lax.all_to_all(updated, axes, split_axis=1, concat_axis=0, tiled=True)  41 us
    pallas_call x2, Pallas kernels, bias_call(): pl.pallas_call(bias_kernel, grid=(rows,), in_specs=[pl.BlockSpec((1, N, C...  12.3 us
  transfers between devices with their start and end apart: 3, of which 3 were waited for; matrix products, arithmetic and copies ran while one was open for 0% of the time, Pallas kernels for 12%

profile of v1, /device:TPU:1, one launch (start us, length us, event | category | flops | bytes accessed | tf_op | source)
XLA Modules:
  0.0 351.6 jit_solution(4706893851515050630)
XLA Ops:
  6.5 0.0 all-gather.3.cloned.1.call-start
  6.5 0.7 multiply_bitcast_fusion.1
  7.2 0.6 pad.7.weight_ref
  7.8 6.1 %bias.2 = f32[6,24,128]{2,1,0:T(8,128)} custom-call(f32[6,768,128]{2,1,0:T(8,128)} %z_ref.5, f32[8,128]{1,0:T(8,128)} %pad.7.weight_ref), custom_call_target="tpu_custom_call" | custom-call | flops 11796480 | bytes 2359296 | tf_op jit(solution)/shard_map/bias/pallas_call | solution.py:40
  13.9 0.0 all-gather.3.cloned.1.call-update
  14.6 0.0 copy-start.3
  14.6 0.9 copy-done.3
  15.6 0.0 copy-start.1
  15.6 21.5 %project.2 = (bf16[6,4,768,128]{3,2,1,0:T(8,128)(2,1)}, bf16[6,4,768,128]{3,2,1,0:T(8,128)(2,1)}, bf16[6,4,768,128]{3,2,1,0:T(8,128)(2,1)}, f32[6,768,128]{2,1,0:T(8,128)S(1)}) custom-call(s32[1]{0:T(128)S(6)} %copy.16.valid_ref, f32[6,768,128]{2,1,0:T(8,128)} %z_ref.5, f32[4,128,128]{2,1,0:T(8,128)S(1)} %copy-done.3), custom_call_target="tpu_custom_call" | custom-call | flops 7851737088 | bytes 18874368 | tf_op jit(solution)/shard_map/project/pallas_call | solution.py:120
  37.1 0.0 copy-start
  37.1 1.4 copy-done
  38.5 50.2 %all-gather.3.cloned.1.call-done.bias_ref = f32[18432,128]{1,0:T(8,128)} async-done(((f32[144,128]{1,0:T(8,128)}), f32[18432,128]{1,0:T(8,128)}) %all-gather.3.cloned.1.call-update) | async-done | bytes 9437200 | tf_op jit(solution)/shard_map/all_gather | solution.py:246
  88.7 0.0 copy-done.1
  88.7 62.6 %attend.2 = f32[6,768,128]{2,1,0:T(8,128)S(1)} custom-call(s32[1]{0:T(128)S(6)} %copy.16.valid_ref, bf16[6,4,768,128]{3,2,1,0:T(8,128)(2,1)} %get-tuple-element.13.q_ref, bf16[6,4,768,128]{3,2,1,0:T(8,128)(2,1)} %get-tuple-element.14.k_ref, bf16[6,4,768,128]{3,2,1,0:T(8,128)(2,1)} %get-tuple-element.15.v_ref, f32[6,768,128]{2,1,0:T(8,128)} %copy-done, ...), custom_call_target="tpu_custom_call" | custom-call | flops 3623878656 | bytes 18874368 | tf_op jit(solution)/shard_map/attend/pallas_call | solution.py:209
  151.3 3.1 copy.11
  154.4 0.0 copy-start.5
  154.4 5.4 %all-to-all-start = ((f32[6,768,128]{2,0,1:T(8,128)}), f32[6,768,128]{2,0,1:T(8,128)S(1)}, u32[]{:S(2)}, u32[]{:S(2)}) async-start(f32[6,768,128]{2,0,1:T(8,128)} %copy.11), calls=%async_computation | async-start | bytes 6291456 | tf_op jit(solution)/shard_map/all_to_all | solution.py:251
  159.8 0.0 all-gather.5.cloned.1.call-start
  159.8 0.0 copy-done.5
  159.9 0.6 pad.8.weight_ref
  160.5 41.0 %all-to-all-done = f32[6,768,128]{2,0,1:T(8,128)S(1)} async-done(((f32[6,768,128]{2,0,1:T(8,128)}), f32[6,768,128]{2,0,1:T(8,128)S(1)}, u32[]{:S(2)}, u32[]{:S(2)}) %all-to-all-start) | async-done | bytes 2359328 | tf_op jit(solution)/shard_map/all_to_all | solution.py:251
  201.5 1.8 copy.13
  203.3 0.0 copy-start.4
  203.3 4.1 %all_to_all.16 = f32[768,6,128]{2,0,1:T(8,128)} reshape(f32[128,6,6,128]{3,1,0,2:T(8,128)} %copy.13) | data formatting | bytes 4718592 | tf_op jit(solution)/shard_map/all_to_all | solution.py:251
  207.4 6.1 %bias.3 = f32[6,24,128]{2,1,0:T(8,128)} custom-call(f32[6,768,128]{2,1,0:T(8,128)} %bitcast.13, f32[8,128]{1,0:T(8,128)} %pad.8.weight_ref), custom_call_target="tpu_custom_call" | custom-call | flops 11796480 | bytes 2359296 | tf_op jit(solution)/shard_map/bias/pallas_call | solution.py:40
  213.6 0.0 all-gather.5.cloned.1.call-update
  213.6 0.0 copy-done.4
  213.6 0.0 copy-start.2
  213.6 21.5 %project.3 = (bf16[6,4,768,128]{3,2,1,0:T(8,128)(2,1)}, bf16[6,4,768,128]{3,2,1,0:T(8,128)(2,1)}, bf16[6,4,768,128]{3,2,1,0:T(8,128)(2,1)}, f32[6,768,128]{2,1,0:T(8,128)S(1)}) custom-call(s32[1]{0:T(128)S(6)} %copy.16.valid_ref, f32[6,768,128]{2,1,0:T(8,128)} %bitcast.14, f32[4,128,128]{2,1,0:T(8,128)S(1)} %copy-done.4), custom_call_target="tpu_custom_call" | custom-call | flops 7851737088 | bytes 18874368 | tf_op jit(solution)/shard_map/project/pallas_call | solution.py:120
  235.1 46.2 %all-gather.5.cloned.1.call-done.bias_ref = f32[18432,128]{1,0:T(8,128)} async-done(((f32[144,128]{1,0:T(8,128)}), f32[18432,128]{1,0:T(8,128)}) %all-gather.5.cloned.1.call-update) | async-done | bytes 9437200 | tf_op jit(solution)/shard_map/all_gather | solution.py:246
  281.3 0.0 copy-done.2
  281.3 63.4 %attend.3 = f32[6,768,128]{2,1,0:T(8,128)} custom-call(s32[1]{0:T(128)S(6)} %copy.16.valid_ref, bf16[6,4,768,128]{3,2,1,0:T(8,128)(2,1)} %get-tuple-element.17.q_ref, bf16[6,4,768,128]{3,2,1,0:T(8,128)(2,1)} %get-tuple-element.18.k_ref, bf16[6,4,768,128]{3,2,1,0:T(8,128)(2,1)} %get-tuple-element.19.v_ref, f32[6,768,128]{2,1,0:T(8,128)S(1)} %get-tuple-element.20.g_ref, ...), custom_call_target="tpu_custom_call" | custom-call | flops 3623878656 | bytes 18874368 | tf_op jit(solution)/shard_map/attend/pallas_call | solution.py:209
  (1 shorter events, 0.0 us)
Async XLA Ops:
  6.5 82.1 %all-gather.3.cloned.1.call-start = ((), (), s32[]{:S(2)}) async-start(), calls=%async_computation.1 | async-start | bytes 9510912 | tf_op jit(solution)/shard_map/all_gather | solution.py:246
  14.6 1.0 copy-start.3
  15.6 73.1 %copy-start.1 = (f32[128,128]{1,0:T(8,128)S(1)}, f32[128,128]{1,0:T(8,128)}, u32[]{:S(2)}) copy-start(f32[128,128]{1,0:T(8,128)} %o_ref.2) | copy-start | bytes 196612
  37.1 1.4 copy-start
  154.4 5.4 %copy-start.5 = (f32[128,4]{0,1:T(4,128)S(1)}, f32[128,4]{0,1:T(4,128)}, u32[]{:S(2)}) copy-start(f32[128,4]{0,1:T(4,128)} %param.15) | copy-start | bytes 6148
  154.4 47.1 %all-to-all-start = ((f32[6,768,128]{2,0,1:T(8,128)}), f32[6,768,128]{2,0,1:T(8,128)S(1)}, u32[]{:S(2)}, u32[]{:S(2)}) async-start(f32[6,768,128]{2,0,1:T(8,128)} %copy.11), calls=%async_computation | async-start | bytes 6291456 | tf_op jit(solution)/shard_map/all_to_all | solution.py:251
  159.8 121.5 %all-gather.5.cloned.1.call-start = ((), (), s32[]{:S(2)}) async-start(), calls=%async_computation.2 | async-start | bytes 9510912 | tf_op jit(solution)/shard_map/all_gather | solution.py:246
  203.3 10.3 %copy-start.4 = (f32[4,128,128]{2,1,0:T(8,128)S(1)}, f32[4,128,128]{2,1,0:T(8,128)}, u32[]{:S(2)}) copy-start(f32[4,128,128]{2,1,0:T(8,128)} %p_ref.3) | copy-start | bytes 786436
  213.6 67.7 %copy-start.2 = (f32[128,128]{1,0:T(8,128)S(1)}, f32[128,128]{1,0:T(8,128)}, u32[]{:S(2)}) copy-start(f32[128,128]{1,0:T(8,128)} %o_ref.3) | copy-start | bytes 196612
Sparse Core Ops, SparseCore 0:
  14.1 74.5 all-gather.2
  213.7 67.5 all-gather.4

commit v2 on v1

--- a/solution.py
+++ b/solution.py
@@ -138,12 +138,13 @@
     )(valid_count, z, projection)
 
 
-def attend_kernel(QC, KT, valid_ref, q_ref, k_ref, v_ref, g_ref, z_ref, bias_ref, o_ref, out_ref,
-                  bias_s, acc_s, o_s):
-    lane = lax.broadcasted_iota(jnp.int32, (1, C), 1)
-    group = lane // D
-
-    @pl.when((pl.program_id(0) == 0) & (pl.program_id(1) == 0))
+def attend_kernel(rows, QC, KT, transposed, valid_ref, q_ref, k_ref, v_ref, g_ref, z_ref, bias_ref, o_ref,
+                  out_ref, bias_s, acc_s, o_s):
+    group = lax.broadcasted_iota(jnp.int32, (1, C), 1) // D
+    chunk, row = pl.program_id(0), pl.program_id(1)
+    per = N // 128 * H
+
+    @pl.when((chunk == 0) & (row == 0))
     def _():
         high, low = halves(o_ref[...])
         o_s[0, :C] = high
@@ -151,13 +152,39 @@
         o_s[1, :C] = low
         o_s[1, C:] = low
 
-    @pl.when(pl.program_id(1) == 0)
-    def _():
-        for block in range(N // 128):
-            for head in range(H):
-                bias_s[head, :, block * 128 : (block + 1) * 128] = bias_ref[
-                    pl.ds(block * H + head, QC, stride=N // 128 * H), :
-                ]
+    @pl.when(row == 0)
+    def _():
+        for head in range(H):
+            for block in range(N // 128):
+                at = pl.ds(block * 128, 128)
+                if transposed:
+                    for part in range(QC // 128):
+                        first = block * 128 * per + (chunk * (QC // 128) + part) * H + head
+                        tile = bias_ref[pl.ds(first, 128, stride=per), :]
+                        bias_s[head, pl.ds(part * 128, 128), at] = tile.T
+                else:
+                    bias_s[head, :, at] = bias_ref[pl.ds(block * H + head, QC, stride=per), :]
+
+    def finish():
+        slot = (row + 1) % 2
+        value = low_value = total = None
+        for head in range(H):
+            acc = acc_s[slot, head]
+            if head == 0:
+                value = low_value = total = acc
+            else:
+                value = jnp.where(group == head, acc, value)
+                low_value = jnp.where(group == (head + 1) % H, acc, low_value)
+                total = jnp.where(group == (head + 2) % H, acc, total)
+        value = value + pltpu.roll(low_value, 3 * D, 1)
+        mixed = value / pltpu.roll(total, 2 * D, 1) * g_ref[0]
+        high, low = halves(mixed)
+        both = jnp.concatenate([high, low], axis=1)
+        out_ref[0] = (
+            z_ref[0]
+            + jnp.dot(both, o_s[0], preferred_element_type=F32)
+            + jnp.dot(both, o_s[1], preferred_element_type=F32)
+        )
 
     def run(keys):
         for head in range(H):
@@ -176,59 +203,56 @@
                     low, v, preferred_element_type=F32
                 )
                 acc = term if acc is None else acc + term
-            acc_s[head] = acc
+            acc_s[row % 2, head] = acc
 
     count = (valid_ref[0] + 127) // 128
     for blocks in range(3, N // 128 + 1):
 
-        @pl.when(count == blocks)
+        @pl.when((count == blocks) & (row < rows))
         def _():
             run(blocks * 128)
-
-    mixed = None
-    for head in range(H):
-        acc = acc_s[head]
-        total = pltpu.roll(acc, 2 * D, 1)
-        value = (acc + pltpu.roll(acc, 3 * D, 1)) / jnp.where(group == head, total, 1.0)
-        mixed = value if mixed is None else jnp.where(group == head, value, mixed)
-    high, low = halves(mixed * g_ref[0])
-    both = jnp.concatenate([high, low], axis=1)
-    out_ref[0] = (
-        z_ref[0]
-        + jnp.dot(both, o_s[0], preferred_element_type=F32)
-        + jnp.dot(both, o_s[1], preferred_element_type=F32)
-    )
-
-
-def attend_call(q, k, v, g, z, bias, out_weight, valid_count, QC=256, KT=256):
+            finish()
+
+    @pl.when(row == rows)
+    def _():
+        finish()
+
+
+def attend_call(q, k, v, g, z, bias, out_weight, valid_count, QC=384, KT=256, transposed=False):
     rows = z.shape[0]
     queries = z.shape[1]
     per = N // 128 * H
-    key_spec = pl.BlockSpec((1, H, N, C), lambda c, r, s: (r, 0, 0, 0))
-    row_spec = pl.BlockSpec((1, QC, C), lambda c, r, s: (r, c, 0))
+    now = lambda r: jnp.minimum(r, rows - 1)
+    last = lambda r: jnp.maximum(r - 1, 0)
+    key_spec = pl.BlockSpec((1, H, N, C), lambda c, r, s: (now(r), 0, 0, 0))
+    row_spec = pl.BlockSpec((1, QC, C), lambda c, r, s: (last(r), c, 0))
+    if transposed:
+        bias_spec = pl.BlockSpec((N * per, 128), lambda c, r, s: (0, 0))
+    else:
+        bias_spec = pl.BlockSpec((QC * per, 128), lambda c, r, s: (c, 0))
     return pl.pallas_call(
-        functools.partial(attend_kernel, QC, KT),
+        functools.partial(attend_kernel, rows, QC, KT, transposed),
         grid_spec=pltpu.PrefetchScalarGridSpec(
             num_scalar_prefetch=1,
-            grid=(queries // QC, rows),
+            grid=(queries // QC, rows + 1),
             in_specs=[
-                pl.BlockSpec((1, H, QC, C), lambda c, r, s: (r, 0, c, 0)),
+                pl.BlockSpec((1, H, QC, C), lambda c, r, s: (now(r), 0, c, 0)),
                 key_spec,
                 key_spec,
                 row_spec,
                 row_spec,
-                pl.BlockSpec((QC * per, 128), lambda c, r, s: (c, 0)),
+                bias_spec,
                 pl.BlockSpec((C, C), lambda c, r, s: (0, 0)),
             ],
             out_specs=row_spec,
             scratch_shapes=[
                 pltpu.VMEM((H, QC, N), F32),
-                pltpu.VMEM((H, QC, C), F32),
+                pltpu.VMEM((2, H, QC, C), F32),
                 pltpu.VMEM((2, 2 * C, C), BF),
             ],
         ),
         out_shape=jax.ShapeDtypeStruct(z.shape, F32),
-        compiler_params=pltpu.CompilerParams(vmem_limit_bytes=50 * 2**20),
+        compiler_params=pltpu.CompilerParams(vmem_limit_bytes=56 * 2**20),
         cost_estimate=pl.CostEstimate(
             flops=rows * queries * N * H * 64 * 4, bytes_accessed=rows * N * C * 4 * 8, transcendentals=0
         ),
@@ -241,16 +265,17 @@
 ):
     axes = ("row", "col")
 
-    def block(z, projection, out_weight, bias_weight):
-        local = bias_call(z, bias_weight).reshape(-1, 128)
-        bias = lax.all_gather(local, axes, axis=0, tiled=True)
-        q, k, v, g = project_call(z, projection, valid_count)
-        return attend_call(q, k, v, g, z, bias, out_weight, valid_count)
-
-    updated = block(pair_rows, start_proj, start_out, start_bias)
+    def gather_bias(z, bias_weight):
+        return lax.all_gather(bias_call(z, bias_weight).reshape(-1, 128), axes, axis=0, tiled=True)
+
+    start_gathered = gather_bias(pair_rows, start_bias)
+    q, k, v, g = project_call(pair_rows, start_proj, valid_count)
+    updated = attend_call(q, k, v, g, pair_rows, start_gathered, start_out, valid_count, N)
+    end_gathered = gather_bias(updated, end_bias)
     columns = lax.all_to_all(updated, axes, split_axis=1, concat_axis=0, tiled=True)
     turned = jnp.swapaxes(columns, 0, 1)
-    return block(turned, end_proj, end_out, end_bias)
+    q, k, v, g = project_call(turned, end_proj, valid_count)
+    return attend_call(q, k, v, g, turned, end_gathered, end_out, valid_count, N, transposed=True)
 
 
 def solution(mesh):

time: 352 us -> 273 us (0.78); the launches traced: 352 us -> 268 us
  waiting for transfers between devices: 137 us -> 68.6 us
  Pallas kernels: 181 us -> 128 us
  blocking collectives: 0 us -> 47.7 us
  starting transfers between devices: 5.42 us -> 0.04 us
  local copies, waits for them, and re-layouts: 12.6 us -> 8.26 us
    pallas_call x2, Pallas kernels: 126 us -> 72.2 us  [attend_call(): pl.pallas_call(functools.partial(attend_kernel, rows, QC, KT, transposed)...]
    all_to_all x0 -> x1, blocking collectives: none -> 47.7 us  [per_device(): lax.all_to_all(updated, axes, split_axis=1, concat_axis=0, tiled=True)]
    all_to_all x1 -> x0, waiting for transfers between devices: 41 us -> none  [per_device(): lax.all_to_all(updated, axes, split_axis=1, concat_axis=0, tiled=True)]
    all_gather x2, waiting for transfers between devices: 96.4 us -> 68.6 us  [gather_bias(): lax.all_gather(bias_call(z, bias_weight).reshape(-1, 128), axes, axis=0,...]
    all_to_all x1 -> x0, starting transfers between devices: 5.38 us -> none  [per_device(): lax.all_to_all(updated, axes, split_axis=1, concat_axis=0, tiled=True)]
    all_to_all x2, local copies, waits for them, and re-layouts: 5.96 us -> 1.8 us  [per_device(): lax.all_to_all(updated, axes, split_axis=1, concat_axis=0, tiled=True)]
  transfers between devices with their start and end apart: 3 -> 2, of which waited for: 3 -> 2; matrix products, arithmetic and copies ran while one was open for 0% -> 1% of each run, Pallas kernels for 12% -> 16%
where the time goes in v2:
time: 273 us; the launch traced here: 268 us
  Pallas kernels  128 us (47%)
  waiting for transfers between devices  68.6 us (25%)
  blocking collectives  47.7 us (17%)
  between operations  14.3 us (5%)
  local copies, waits for them, and re-layouts  8.26 us (3%)
    pallas_call x2, Pallas kernels, attend_call(): pl.pallas_call(functools.partial(attend_kernel, rows, QC, KT, transposed)...  72.2 us
    all_gather x2, waiting for transfers between devices, gather_bias(): lax.all_gather(bias_call(z, bias_weight).reshape(-1, 128), axes, axis=0,...  68.6 us
    all_to_all x1, blocking collectives, per_device(): lax.all_to_all(updated, axes, split_axis=1, concat_axis=0, tiled=True)  47.7 us
    pallas_call x2, Pallas kernels, project_call(): pl.pallas_call(project_kernel, grid_spec=pltpu.PrefetchScalarGridSpec(num...  42.9 us
    pallas_call x2, Pallas kernels, bias_call(): pl.pallas_call(bias_kernel, grid=(rows,), in_specs=[pl.BlockSpec((1, N, C...  12.4 us
  transfers between devices with their start and end apart: 2, of which 2 were waited for; matrix products, arithmetic and copies ran while one was open for 1% of the time, Pallas kernels for 16%

profile of v2, /device:TPU:1, one launch (start us, length us, event | category | flops | bytes accessed | tf_op | source)
XLA Modules:
  0.0 267.8 jit_solution(16784172949383744922)
XLA Ops:
  6.5 0.0 all-gather.3.cloned.1.call-start
  6.5 0.7 multiply_bitcast_fusion.1
  7.2 0.6 pad.7.weight_ref
  7.8 6.1 %bias.2 = f32[6,24,128]{2,1,0:T(8,128)} custom-call(f32[6,768,128]{2,1,0:T(8,128)} %z_ref.5, f32[8,128]{1,0:T(8,128)} %pad.7.weight_ref), custom_call_target="tpu_custom_call" | custom-call | flops 11796480 | bytes 2359296 | tf_op jit(solution)/shard_map/bias/pallas_call | solution.py:40
  14.0 0.0 all-gather.3.cloned.1.call-update
  14.0 0.0 all-gather.5.cloned.1.call-start
  14.7 0.7 multiply_bitcast_fusion
  15.4 0.6 pad.8.weight_ref
  16.0 0.0 copy-start.2
  16.0 0.9 copy-done.2
  16.9 21.5 %project.2 = (bf16[6,4,768,128]{3,2,1,0:T(8,128)(2,1)}, bf16[6,4,768,128]{3,2,1,0:T(8,128)(2,1)}, bf16[6,4,768,128]{3,2,1,0:T(8,128)(2,1)}, f32[6,768,128]{2,1,0:T(8,128)S(1)}) custom-call(s32[1]{0:T(128)S(6)} %copy.16.valid_ref, f32[6,768,128]{2,1,0:T(8,128)} %z_ref.5, f32[4,128,128]{2,1,0:T(8,128)S(1)} %copy-done.2), custom_call_target="tpu_custom_call" | custom-call | flops 7851737088 | bytes 18874368 | tf_op jit(solution)/shard_map/project/pallas_call | solution.py:120
  38.4 0.0 copy-start.1
  38.4 1.4 copy-done.1
  39.8 48.9 %all-gather.3.cloned.1.call-done.bias_ref = f32[18432,128]{1,0:T(8,128)} async-done(((f32[144,128]{1,0:T(8,128)}), f32[18432,128]{1,0:T(8,128)}) %all-gather.3.cloned.1.call-update) | async-done | bytes 9437200 | tf_op jit(solution)/shard_map/all_gather | solution.py:269
  88.7 36.1 %attend.2.z_ref = f32[6,768,128]{2,1,0:T(8,128)} custom-call(s32[1]{0:T(128)S(6)} %copy.16.valid_ref, bf16[6,4,768,128]{3,2,1,0:T(8,128)(2,1)} %get-tuple-element.13.q_ref, bf16[6,4,768,128]{3,2,1,0:T(8,128)(2,1)} %get-tuple-element.14.k_ref, bf16[6,4,768,128]{3,2,1,0:T(8,128)(2,1)} %get-tuple-element.15.v_ref, f32[6,768,128]{2,1,0:T(8,128)} %copy-done.1, ...), custom_call_target="tpu_custom_call" | custom-call | flops 3623878656 | bytes 18874368 | tf_op jit(solution)/shard_map/attend/pallas_call | solution.py:233
  124.8 0.0 copy-start.4
  124.8 6.3 %bias.3 = f32[6,24,128]{2,1,0:T(8,128)} custom-call(f32[6,768,128]{2,1,0:T(8,128)} %attend.2.z_ref, f32[8,128]{1,0:T(8,128)} %pad.8.weight_ref), custom_call_target="tpu_custom_call" | custom-call | flops 11796480 | bytes 2359296 | tf_op jit(solution)/shard_map/bias/pallas_call | solution.py:40
  131.1 0.0 all-gather.5.cloned.1.call-update
  131.1 0.0 copy-done.4
  131.2 1.4 copy.11
  132.6 47.7 %all_to_all.18 = f32[6,768,128]{2,0,1:T(8,128)S(1)} all-to-all(f32[6,768,128]{2,0,1:T(8,128)S(1)} %copy.11), channel_id=1, replica_groups=mesh['row'=8,'col'=16] {'row','col'}, dimensions={1} | all-to-all | bytes 4718592 | tf_op jit(solution)/shard_map/all_to_all | solution.py:275
  180.2 0.2 copy.13
  180.5 0.0 copy-start.3
  180.5 1.6 all_to_all.16
  182.1 0.0 copy-done.3
  182.1 21.5 %project.3 = (bf16[6,4,768,128]{3,2,1,0:T(8,128)(2,1)}, bf16[6,4,768,128]{3,2,1,0:T(8,128)(2,1)}, bf16[6,4,768,128]{3,2,1,0:T(8,128)(2,1)}, f32[6,768,128]{2,1,0:T(8,128)S(1)}) custom-call(s32[1]{0:T(128)S(6)} %copy.16.valid_ref, f32[6,768,128]{2,1,0:T(8,128)} %bitcast.14, f32[4,128,128]{2,1,0:T(8,128)S(1)} %copy-done.3), custom_call_target="tpu_custom_call" | custom-call | flops 7851737088 | bytes 18874368 | tf_op jit(solution)/shard_map/project/pallas_call | solution.py:120
  203.5 0.0 copy-start
  203.5 1.5 copy-done
  205.0 19.7 %all-gather.5.cloned.1.call-done.bias_ref = f32[18432,128]{1,0:T(8,128)} async-done(((f32[144,128]{1,0:T(8,128)}), f32[18432,128]{1,0:T(8,128)}) %all-gather.5.cloned.1.call-update) | async-done | bytes 9437200 | tf_op jit(solution)/shard_map/all_gather | solution.py:269
  224.7 36.0 %attend.3 = f32[6,768,128]{2,1,0:T(8,128)} custom-call(s32[1]{0:T(128)S(6)} %copy.16.valid_ref, bf16[6,4,768,128]{3,2,1,0:T(8,128)(2,1)} %get-tuple-element.17.q_ref, bf16[6,4,768,128]{3,2,1,0:T(8,128)(2,1)} %get-tuple-element.18.k_ref, bf16[6,4,768,128]{3,2,1,0:T(8,128)(2,1)} %get-tuple-element.19.v_ref, f32[6,768,128]{2,1,0:T(8,128)} %copy-done, ...), custom_call_target="tpu_custom_call" | custom-call | flops 3623878656 | bytes 18874368 | tf_op jit(solution)/shard_map/attend/pallas_call | solution.py:233
Async XLA Ops:
  6.5 82.1 %all-gather.3.cloned.1.call-start = ((), (), s32[]{:S(2)}) async-start(), calls=%async_computation.1 | async-start | bytes 9510912 | tf_op jit(solution)/shard_map/all_gather | solution.py:269
  14.0 210.7 %all-gather.5.cloned.1.call-start = ((), (), s32[]{:S(2)}) async-start(), calls=%async_computation.2 | async-start | bytes 9510912 | tf_op jit(solution)/shard_map/all_gather | solution.py:269
  16.0 0.9 copy-start.2
  38.4 1.4 copy-start.1
  124.8 6.3 %copy-start.4 = (f32[6,768,128]{2,1,0:T(8,128)S(1)}, f32[6,768,128]{2,1,0:T(8,128)}, u32[]{:S(2)}) copy-start(f32[6,768,128]{2,1,0:T(8,128)} %attend.2.z_ref) | copy-start | bytes 7077892
  180.5 1.6 copy-start.3
  203.5 1.5 copy-start
Sparse Core Ops, SparseCore 0:
  14.1 74.5 all-gather.2
  131.3 93.4 all-gather.4
